TPU v7x, 32 devices: a whole 2x2x4 slice. The times are simulated.
32 devices in a mesh: polar: 8 (over y, x, core), azimuth: 4 (over z).
Axes of the slice: x: 2, y: 2, z: 4, core: 2. Of those that a mesh axis runs over, the one named last changes fastest.
Arguments:
- grid_input: bfloat16 [720, 276480], P('polar', 'azimuth'), may hold values from -6 to 6
- cotangent: bfloat16 [720, 192, 1440], P('polar', 'azimuth'), may hold values from -6 to 6
- forward_legendre: bfloat16 [720, 256, 256], P(None, 'polar'), may hold values from -0.21875 to 0.21875
- inverse_legendre: bfloat16 [720, 256, 256], P(None, 'polar'), may hold values from -0.375 to 0.375
- filter_weight: bfloat16 [256, 73728], P('polar'), may hold values from -0.3125 to 0.3125
Outputs:
- filtered: bfloat16 [720, 192, 1440], P('polar', 'azimuth')
- grid_grad: bfloat16 [720, 276480], P('polar', 'azimuth')
All inputs are finite; a program needn't handle non-finite values.
Results may differ from a plain program's by a relative error of at most 0.02.
Values may be sent and summed in bfloat16 or wider, within the bound.
A program may use at most 256 MiB of HBM per device.

v0:
```python
import math

import jax
import jax.numpy as jnp
from jax import lax
from jax.sharding import PartitionSpec as P

LON = 1440
C = 192
ORDERS = 256


def make_tables():
    longitude = jnp.arange(LON, dtype=jnp.int32)
    order_index = jnp.arange(ORDERS, dtype=jnp.int32)
    phases = (longitude[:, None] * order_index[None, :] % LON).astype(jnp.float32)
    angles = phases * (2.0 * math.pi / LON)
    factor = 1.0 / math.sqrt(LON)
    stacked = jnp.stack([jnp.cos(angles) * factor, -jnp.sin(angles) * factor], axis=-1)
    doubling = jnp.where(order_index == 0, 1.0, 2.0).astype(jnp.float32)
    basis_plain = stacked.reshape(LON, 2 * ORDERS).astype(jnp.bfloat16)
    basis_doubled = (
        (stacked * doubling[None, :, None]).reshape(LON, 2 * ORDERS).astype(jnp.bfloat16)
    )
    return (basis_plain, basis_doubled)


def to_spectrum(segment, basis_plain):
    product = jnp.einsum("alc,lj->ajc", segment, basis_plain, preferred_element_type=jnp.float32)
    return product.astype(jnp.bfloat16).reshape(segment.shape[0], ORDERS, 2, segment.shape[2])


def mix_forward(modes, kernel):
    shape_in = modes.shape
    flat = modes.reshape(shape_in[0], shape_in[1], 2 * shape_in[3])
    result = jnp.einsum("lmk,lkj->lmj", flat, kernel, preferred_element_type=jnp.float32)
    return result.astype(jnp.bfloat16).reshape(shape_in)


def mix_adjoint(modes, kernel):
    shape_in = modes.shape
    flat = modes.reshape(shape_in[0], shape_in[1], 2 * shape_in[3])
    result = jnp.einsum("lmj,lkj->lmk", flat, kernel, preferred_element_type=jnp.float32)
    return result.astype(jnp.bfloat16).reshape(shape_in)


def to_modes(coefficients):
    return lax.all_to_all(coefficients, "azimuth", split_axis=1, concat_axis=3, tiled=True)


def from_modes(mixed_modes):
    return lax.all_to_all(mixed_modes, "azimuth", split_axis=3, concat_axis=1, tiled=True)


def degree_sum_local(field, table):
    columns = lax.all_to_all(field, "polar", split_axis=1, concat_axis=0, tiled=True)
    blocks = lax.axis_size("polar")
    row_count = columns.shape[0] // blocks
    split_field = columns.reshape(blocks, row_count, columns.shape[1], 2, columns.shape[3])
    split_table = table.reshape(blocks, row_count, table.shape[1], table.shape[2])
    partial_sums = jnp.einsum(
        "bamrc,baml->blmrc", split_field, split_table, preferred_element_type=jnp.float32
    )
    rounded = lax.optimization_barrier(partial_sums.astype(jnp.bfloat16))
    summed = jnp.sum(rounded.astype(jnp.float32), axis=0).astype(jnp.bfloat16)
    return lax.all_to_all(summed, "polar", split_axis=0, concat_axis=1, tiled=True)


def degree_rows_local(modes, table):
    all_degrees = lax.all_to_all(modes, "polar", split_axis=1, concat_axis=0, tiled=True)
    grid_rows = jnp.einsum(
        "lmrc,aml->amrc", all_degrees, table, preferred_element_type=jnp.float32
    ).astype(jnp.bfloat16)
    return lax.all_to_all(grid_rows, "polar", split_axis=0, concat_axis=1, tiled=True)


def on_device(grid_input, cotangent, forward_legendre, inverse_legendre, filter_weight):
    basis_plain, basis_doubled = make_tables()
    weight_cube = filter_weight.reshape(filter_weight.shape[0], 2, C, C)
    weight_real = weight_cube[:, 0]
    weight_imag = weight_cube[:, 1]
    upper_rows = jnp.concatenate([weight_real, weight_imag], axis=2)
    lower_rows = jnp.concatenate([-weight_imag, weight_real], axis=2)
    kernel = jnp.concatenate([upper_rows, lower_rows], axis=1)
    grid_cube = grid_input.reshape(grid_input.shape[0], grid_input.shape[1] // C, C)
    spectrum = (lambda segment: to_spectrum(segment, basis_plain))(
        lax.all_to_all(grid_cube, "azimuth", split_axis=2, concat_axis=1, tiled=True)
    )
    lat_rows = cotangent.shape[0]
    chan_rows = cotangent.shape[1]
    grad_synthesis = jnp.einsum(
        "acl,lj->ajc", cotangent, basis_doubled, preferred_element_type=jnp.float32
    )
    grad_synthesis = grad_synthesis.astype(jnp.bfloat16).reshape(lat_rows, ORDERS, 2, chan_rows)
    coefficients = degree_sum_local(spectrum, forward_legendre)
    grad_mixed = degree_sum_local(grad_synthesis, inverse_legendre)
    mixed_modes = from_modes(mix_forward(to_modes(coefficients), kernel))
    grad_coefficients = from_modes(mix_adjoint(to_modes(grad_mixed), kernel))
    synthesis = degree_rows_local(mixed_modes, inverse_legendre)
    grad_spectrum = degree_rows_local(grad_coefficients, forward_legendre)
    filtered = jnp.einsum(
        "ajc,lj->acl",
        synthesis.reshape(lat_rows, 2 * ORDERS, chan_rows),
        basis_doubled,
        preferred_element_type=jnp.float32,
    ).astype(jnp.bfloat16)
    grad_full = jnp.einsum(
        "ajc,lj->alc",
        grad_spectrum.reshape(lat_rows, 2 * ORDERS, chan_rows),
        basis_plain,
        preferred_element_type=jnp.float32,
    ).astype(jnp.bfloat16)
    grid_grad = lax.all_to_all(grad_full, "azimuth", split_axis=1, concat_axis=2, tiled=True)
    return (
        filtered,
        grid_grad.reshape(grid_grad.shape[0], grid_grad.shape[1] * grid_grad.shape[2]),
    )


def solution(mesh):
    return jax.shard_map(
        on_device,
        mesh=mesh,
        in_specs=(
            P("polar", "azimuth"),
            P("polar", "azimuth", None),
            P(None, "polar", None),
            P(None, "polar", None),
            P("polar", None),
        ),
        out_specs=(P("polar", "azimuth", None), P("polar", "azimuth")),
        check_vma=False,
    )
```

profile of v0, /device:TPU:0, one launch (start us, length us, event | category | flops | bytes accessed | tf_op | source)
XLA Modules:
  0.0 1608.9 jit_solution(18274176505586582638)
XLA Ops:
  0.6 19.0 %reshape.164 = bf16[90,360,192]{2,1,0:T(8,128)(2,1)} reshape(bf16[90,69120]{1,0:T(8,128)(2,1)} %param.5) | data formatting | bytes 24883200 | tf_op jit(solution)/shard_map/reshape | solution.py:85
  19.6 23.2 %copy.182 = bf16[90,360,192]{1,0,2:T(8,128)(2,1)} copy(bf16[90,360,192]{2,1,0:T(8,128)(2,1)} %reshape.164) | data formatting | bytes 24883200 | tf_op jit(solution)/shard_map/reshape | solution.py:85
  69.2 37.9 %convert_bitcast_fusion.4 = bf16[90,512,48]{1,0,2:T(8,128)(2,1)} fusion(bf16[90,48,1440]{2,1,0:T(8,128)(2,1)} %param.6, f32[1440,512]{0,1:T(8,128)} %stack.8, f32[512]{0:T(512)S(1)} %mul.103), kind=kOutput, calls=%fused_computation.17 | convolution fusion | flops 6373785600 | bytes 19816448 | tf_op jit(solution)/shard_map/acl,lj->ajc/dot_general | solution.py:91
  107.1 8.5 copy.212
  115.6 242.3 %all-to-all-done = bf16[90,360,192]{1,0,2:T(8,128)(2,1)} async-done(((bf16[90,360,192]{1,0,2:T(8,128)(2,1)}), bf16[90,360,192]{1,0,2:T(8,128)(2,1)}, u32[]{:S(2)}, u32[]{:S(2)}) %all-to-all-start) | async-done | bytes 12441632 | tf_op jit(solution)/shard_map/all_to_all | solution.py:87
  369.0 18.6 %copy.245 = bf16[90,4,360,48]{2,1,0,3:T(4,128)(2,1)} copy(bf16[90,4,360,48]{2,0,3,1:T(8,128)(2,1)} %bitcast.3) | data formatting | bytes 24883200 | tf_op jit(solution)/shard_map/all_to_all | solution.py:87
  387.6 23.5 %reshape.185 = bf16[90,1440,48]{1,0,2:T(8,128)(2,1)} reshape(bf16[90,4,360,48]{2,1,0,3:T(4,128)(2,1)} %copy.245) | data formatting | bytes 24883200 | tf_op jit(solution)/shard_map/all_to_all | solution.py:87
  411.0 14.2 convert_bitcast_fusion.6
  425.2 8.4 copy.187
  439.0 18.1 %convert_bitcast_fusion.1 = bf16[8,256,32,2,48]{1,4,3,2,0:T(8,128)(2,1)} fusion(bf16[8,90,32,2,48]{1,4,3,2,0:T(8,128)(2,1)} %bitcast.37, bf16[8,90,32,256,1]{3,2,1,0,4:T(8,128)(2,1)} %bitcast.138), kind=kOutput, calls=%fused_computation.8 | convolution fusion | flops 1138753536 | bytes 28803072 | tf_op jit(solution)/shard_map/bamrc,baml->blmrc/dot_general | solution.py:61
  471.4 8.9 reshape.196
  480.4 30.2 %all-to-all-done.1 = bf16[90,256,2,48]{0,3,2,1:T(8,128)(2,1)} async-done(((bf16[90,256,2,48]{0,3,2,1:T(8,128)(2,1)}), bf16[90,256,2,48]{0,3,2,1:T(8,128)(2,1)}, u32[]{:S(2)}, u32[]{:S(2)}) %all-to-all-start.1) | async-done | bytes 4423712 | tf_op jit(solution)/shard_map/all_to_all | solution.py:56
  514.4 18.1 %convert_bitcast_fusion.2 = bf16[8,256,32,2,48]{1,4,3,2,0:T(8,128)(2,1)} fusion(bf16[8,90,32,2,48]{1,4,3,2,0:T(8,128)(2,1)} %bitcast.7, bf16[8,90,32,256,1]{3,2,1,0,4:T(8,128)(2,1)} %bitcast.136), kind=kOutput, calls=%fused_computation.9 | convolution fusion | flops 1138753536 | bytes 28803072 | tf_op jit(solution)/shard_map/bamrc,baml->blmrc/dot_general | solution.py:61
  546.8 8.9 reshape.186
  565.6 12.8 copy.264
  578.4 13.0 copy.265
  609.3 12.8 copy.249
  622.0 13.0 copy.250
  648.2 9.6 reshape.168
  670.8 9.6 copy.303
  688.1 9.5 convolution_convert_fusion.1
  703.4 10.0 copy.220
  728.0 9.6 copy.304
  745.3 9.3 convolution_convert_fusion.2
  760.5 10.0 copy.197
  796.9 8.9 reshape.202
  805.9 9.8 all-to-all-done.4
  837.6 8.9 reshape.192
  858.4 12.8 copy.270
  878.8 20.0 %convert_bitcast_fusion.3 = bf16[720,32,2,48]{0,3,2,1:T(8,128)(2,1)} fusion(bf16[256,32,2,48]{0,3,2,1:T(8,128)(2,1)S(1)} %all_to_all.210, bf16[720,32,256,1]{2,1,0,3:T(8,128)(2,1)} %bitcast.137), kind=kOutput, calls=%fused_computation.16 | convolution fusion | flops 1134673920 | bytes 17793024 | tf_op jit(solution)/shard_map/lmrc,aml->amrc/dot_general | solution.py:71
  898.9 26.8 %copy.227 = bf16[720,32,2,48]{3,2,1,0:T(2,128)(2,1)} copy(bf16[720,32,2,48]{0,3,2,1:T(8,128)(2,1)} %convert_bitcast_fusion.3) | data formatting | bytes 8847360 | tf_op jit(solution)/shard_map/convert_element_type | solution.py:73
  925.7 19.0 %reshape.204 = bf16[8,2,138240]{2,1,0:T(2,128)(2,1)} reshape(bf16[720,32,2,48]{3,2,1,0:T(2,128)(2,1)} %copy.227) | data formatting | bytes 8847360
  955.0 12.8 copy.255
  975.3 19.8 %convert_bitcast_fusion.5 = bf16[720,32,2,48]{0,3,2,1:T(8,128)(2,1)} fusion(bf16[256,32,2,48]{0,3,2,1:T(8,128)(2,1)S(1)} %all_to_all.189, bf16[720,32,256,1]{2,1,0,3:T(8,128)(2,1)} %bitcast.139), kind=kOutput, calls=%fused_computation.18 | convolution fusion | flops 1134673920 | bytes 17793024 | tf_op jit(solution)/shard_map/lmrc,aml->amrc/dot_general | solution.py:71
  995.1 26.8 %copy.204 = bf16[720,32,2,48]{3,2,1,0:T(2,128)(2,1)} copy(bf16[720,32,2,48]{0,3,2,1:T(8,128)(2,1)} %convert_bitcast_fusion.5) | data formatting | bytes 8847360 | tf_op jit(solution)/shard_map/convert_element_type | solution.py:73
  1022.0 18.9 %reshape.194 = bf16[8,2,138240]{2,1,0:T(2,128)(2,1)} reshape(bf16[720,32,2,48]{3,2,1,0:T(2,128)(2,1)} %copy.204) | data formatting | bytes 8847360
  1045.5 13.4 reshape.205
  1058.9 27.2 %copy.228 = bf16[8,90,32,2,48]{1,4,3,2,0:T(8,128)(2,1)} copy(bf16[8,90,32,2,48]{4,3,2,1,0:T(2,128)(2,1)} %bitcast.140) | data formatting | bytes 8847360 | tf_op jit(solution)/shard_map/all_to_all | solution.py:74
  1086.2 14.4 convert_bitcast_fusion
  1100.6 22.6 %copy.231 = bf16[90,1440,48]{0,2,1:T(8,128)(2,1)} copy(bf16[90,1440,48]{1,0,2:T(8,128)(2,1)} %convert_bitcast_fusion) | data formatting | bytes 24883200 | tf_op jit(solution)/shard_map/convert_element_type | solution.py:112
  1133.9 13.4 reshape.195
  1147.3 27.1 %copy.205 = bf16[8,90,32,2,48]{1,4,3,2,0:T(8,128)(2,1)} copy(bf16[8,90,32,2,48]{4,3,2,1,0:T(2,128)(2,1)} %bitcast.141) | data formatting | bytes 8847360 | tf_op jit(solution)/shard_map/all_to_all | solution.py:74
  1174.5 9.4 copy.207
  1183.8 330.3 %all-to-all-done.13 = bf16[90,1440,48]{0,2,1:T(8,128)(2,1)} async-done(((bf16[90,1440,48]{0,2,1:T(8,128)(2,1)}), bf16[90,1440,48]{0,2,1:T(8,128)(2,1)}, u32[]{:S(2)}, u32[]{:S(2)}) %all-to-all-start.13) | async-done | bytes 12441632 | tf_op jit(solution)/shard_map/all_to_all | solution.py:113
  1514.1 29.2 %copy.273 = bf16[90,4,360,48]{2,1,3,0:T(4,128)(2,1)} copy(bf16[90,4,360,48]{0,3,2,1:T(8,128)(2,1)} %bitcast.60) | data formatting | bytes 24883200 | tf_op jit(solution)/shard_map/all_to_all | solution.py:113
  1543.2 33.2 %copy.233 = bf16[90,360,4,48]{0,3,2,1:T(8,128)(2,1)} copy(bf16[90,360,4,48]{1,2,3,0:T(4,128)(2,1)} %bitcast.135) | data formatting | bytes 24883200 | tf_op jit(solution)/shard_map/all_to_all | solution.py:113
  1576.5 19.9 %copy.234 = bf16[90,69120]{1,0:T(8,128)(2,1)} copy(bf16[90,69120]{0,1:T(8,128)(2,1)} %bitcast.134) | data formatting | bytes 24883200
  1596.4 12.3 convolution_convert_fusion
  (76 shorter events, 271.8 us)
Async XLA Ops:
  42.8 315.1 %all-to-all-start = ((bf16[90,360,192]{1,0,2:T(8,128)(2,1)}), bf16[90,360,192]{1,0,2:T(8,128)(2,1)}, u32[]{:S(2)}, u32[]{:S(2)}) async-start(bf16[90,360,192]{1,0,2:T(8,128)(2,1)} %copy.182), calls=%async_computation | async-start | bytes 28311552 | tf_op jit(solution)/shard_map/all_to_all | solution.py:87
  357.9 76.4 %all-to-all-start.7 = ((bf16[90,256,2,48]{0,3,2,1:T(8,128)(2,1)}), bf16[90,256,2,48]{0,3,2,1:T(8,128)(2,1)}, u32[]{:S(2)}, u32[]{:S(2)}) async-start(bf16[90,256,2,48]{0,3,2,1:T(8,128)(2,1)} %bitcast.144), calls=%async_computation.7 | async-start | bytes 12582912 | tf_op jit(solution)/shard_map/all_to_all | solution.py:56
  369.0 42.1 %copy-start.4 = (bf16[1440,512]{0,1:T(8,128)(2,1)}, bf16[1440,512]{0,1:T(8,128)(2,1)S(1)}, u32[]{:S(2)}) copy-start(bf16[1440,512]{0,1:T(8,128)(2,1)S(1)} %convert_element_type.103) | copy-start | bytes 4423684
  434.2 76.4 %all-to-all-start.1 = ((bf16[90,256,2,48]{0,3,2,1:T(8,128)(2,1)}), bf16[90,256,2,48]{0,3,2,1:T(8,128)(2,1)}, u32[]{:S(2)}, u32[]{:S(2)}) async-start(bf16[90,256,2,48]{0,3,2,1:T(8,128)(2,1)} %bitcast.145), calls=%async_computation.1 | async-start | bytes 12582912 | tf_op jit(solution)/shard_map/all_to_all | solution.py:56
  510.6 45.1 %all-to-all-start.8 = ((bf16[8,2,49152]{2,1,0:T(2,128)(2,1)}), bf16[8,2,49152]{2,1,0:T(2,128)(2,1)S(1)}, u32[]{:S(2)}, u32[]{:S(2)}) async-start(bf16[8,2,49152]{2,1,0:T(2,128)(2,1)} %reshape.196), calls=%async_computation.8 | async-start | bytes 3145728 | tf_op jit(solution)/shard_map/all_to_all | solution.py:66
  555.7 43.8 %all-to-all-start.2 = ((bf16[8,2,49152]{2,1,0:T(2,128)(2,1)}), bf16[8,2,49152]{2,1,0:T(2,128)(2,1)S(1)}, u32[]{:S(2)}, u32[]{:S(2)}) async-start(bf16[8,2,49152]{2,1,0:T(2,128)(2,1)} %reshape.186), calls=%async_computation.2 | async-start | bytes 3145728 | tf_op jit(solution)/shard_map/all_to_all | solution.py:66
  599.5 43.6 %all-to-all-start.9 = ((bf16[4,2,98304]{2,1,0:T(2,128)(2,1)}), bf16[4,2,98304]{2,1,0:T(2,128)(2,1)S(1)}, u32[]{:S(2)}, u32[]{:S(2)}) async-start(bf16[4,2,98304]{2,1,0:T(2,128)(2,1)} %reshape.198), calls=%async_computation.9 | async-start | bytes 3145728 | tf_op jit(solution)/shard_map/all_to_all | solution.py:48
  643.1 73.7 %all-to-all-start.3 = ((bf16[4,2,98304]{2,1,0:T(2,128)(2,1)}), bf16[4,2,98304]{2,1,0:T(2,128)(2,1)}, u32[]{:S(2)}, u32[]{:S(2)}) async-start(bf16[4,2,98304]{2,1,0:T(2,128)(2,1)} %reshape.188), calls=%async_computation.3 | async-start | bytes 3145728 | tf_op jit(solution)/shard_map/all_to_all | solution.py:48
  657.8 4.9 copy-start
  680.4 7.7 copy-start.2
  716.8 57.4 %all-to-all-start.10 = ((bf16[4,2,98304]{2,1,0:T(2,128)(2,1)}), bf16[4,2,98304]{2,1,0:T(2,128)(2,1)}, u32[]{:S(2)}, u32[]{:S(2)}) async-start(bf16[4,2,98304]{2,1,0:T(2,128)(2,1)} %reshape.200), calls=%async_computation.10 | async-start | bytes 3145728 | tf_op jit(solution)/shard_map/all_to_all | solution.py:52
  737.6 7.7 copy-start.3
  774.2 41.4 %all-to-all-start.4 = ((bf16[4,2,98304]{2,1,0:T(2,128)(2,1)}), bf16[4,2,98304]{2,1,0:T(2,128)(2,1)}, u32[]{:S(2)}, u32[]{:S(2)}) async-start(bf16[4,2,98304]{2,1,0:T(2,128)(2,1)} %reshape.190), calls=%async_computation.4 | async-start | bytes 3145728 | tf_op jit(solution)/shard_map/all_to_all | solution.py:52
  815.6 30.9 %all-to-all-start.11 = ((bf16[8,2,49152]{2,1,0:T(2,128)(2,1)}), bf16[8,2,49152]{2,1,0:T(2,128)(2,1)}, u32[]{:S(2)}, u32[]{:S(2)}) async-start(bf16[8,2,49152]{2,1,0:T(2,128)(2,1)} %reshape.202), calls=%async_computation.11 | async-start | bytes 3145728 | tf_op jit(solution)/shard_map/all_to_all | solution.py:70
  846.5 98.2 %all-to-all-start.5 = ((bf16[8,2,49152]{2,1,0:T(2,128)(2,1)}), bf16[8,2,49152]{2,1,0:T(2,128)(2,1)S(1)}, u32[]{:S(2)}, u32[]{:S(2)}) async-start(bf16[8,2,49152]{2,1,0:T(2,128)(2,1)} %reshape.192), calls=%async_computation.5 | async-start | bytes 3145728 | tf_op jit(solution)/shard_map/all_to_all | solution.py:70
  944.7 96.2 %all-to-all-start.12 = ((bf16[8,2,138240]{2,1,0:T(2,128)(2,1)}), bf16[8,2,138240]{2,1,0:T(2,128)(2,1)}, u32[]{:S(2)}, u32[]{:S(2)}) async-start(bf16[8,2,138240]{2,1,0:T(2,128)(2,1)} %reshape.204), calls=%async_computation.12 | async-start | bytes 8847360 | tf_op jit(solution)/shard_map/all_to_all | solution.py:74
  1040.9 82.3 %all-to-all-start.6 = ((bf16[8,2,138240]{2,1,0:T(2,128)(2,1)}), bf16[8,2,138240]{2,1,0:T(2,128)(2,1)}, u32[]{:S(2)}, u32[]{:S(2)}) async-start(bf16[8,2,138240]{2,1,0:T(2,128)(2,1)} %reshape.194), calls=%async_computation.6 | async-start | bytes 8847360 | tf_op jit(solution)/shard_map/all_to_all | solution.py:74
  1058.9 27.2 %copy-start.5 = (bf16[1440,512]{0,1:T(8,128)(2,1)S(1)}, bf16[1440,512]{0,1:T(8,128)(2,1)}, u32[]{:S(2)}) copy-start(bf16[1440,512]{0,1:T(8,128)(2,1)} %copy-done.4) | copy-start | bytes 4423684
  1123.2 7.6 copy-start.1
  1123.2 390.9 %all-to-all-start.13 = ((bf16[90,1440,48]{0,2,1:T(8,128)(2,1)}), bf16[90,1440,48]{0,2,1:T(8,128)(2,1)}, u32[]{:S(2)}, u32[]{:S(2)}) async-start(bf16[90,1440,48]{0,2,1:T(8,128)(2,1)} %copy.231), calls=%async_computation.13 | async-start | bytes 35389440 | tf_op jit(solution)/shard_map/all_to_all | solution.py:113
where the time goes:
time: 1630 us; the launch traced here: 1610 us
  local copies, waits for them, and re-layouts  724 us (44%)
  waiting for transfers between devices  613 us (38%)
  matrix products  174 us (11%)
  starting transfers between devices  68.3 us (4%)
  other arithmetic  28.5 us (2%)
    all_to_all x1, waiting for transfers between devices, on_device(): lax.all_to_all(grad_full, 'azimuth', split_axis=1, concat_axis=2, tiled=T...  330 us
    all_to_all x1, waiting for transfers between devices, on_device(): lax.all_to_all(grid_cube, 'azimuth', split_axis=2, concat_axis=1, tiled=T...  242 us
    unnamed x33, local copies, waits for them, and re-layouts  191 us
    all_to_all x2, local copies, waits for them, and re-layouts, on_device(): lax.all_to_all(grad_full, 'azimuth', split_axis=1, concat_axis=2, tiled=T...  62.4 us
    all_to_all x2, local copies, waits for them, and re-layouts, degree_rows_local(): lax.all_to_all(grid_rows, 'polar', split_axis=0, concat_axis=1, tiled=True)  54.3 us
    convert_element_type x2, local copies, waits for them, and re-layouts, degree_rows_local(): grid_rows = jnp.einsum('lmrc,aml->amrc', all_degrees, table, preferred_el...  53.7 us
    all_to_all x4, local copies, waits for them, and re-layouts, degree_sum_local(): lax.all_to_all(summed, 'polar', split_axis=0, concat_axis=1, tiled=True)  51.5 us
    reshape x2, local copies, waits for them, and re-layouts, on_device(): grid_input.reshape(grid_input.shape[0], grid_input.shape[1] // C, C)  42.2 us
  transfers between devices with their start and end apart: 14, of which 5 were waited for; matrix products, arithmetic and copies ran while one was open for 48% of the time, Pallas kernels for 0%

commit v1 on v0

v1 whole, which is shorter than its diff:
```python
import math

import jax
import jax.numpy as jnp
import numpy as np
from jax import lax
from jax.experimental import pallas as pl
from jax.experimental.pallas import tpu as pltpu
from jax.sharding import PartitionSpec as P

LON = 1440
C = 192
ORDERS = 256
VMEM_BYTES = 48 * 1024 * 1024


def host_table():
    longitude = np.arange(LON)
    order = np.arange(ORDERS)
    angles = (order[:, None] * longitude[None, :] % LON) * (2.0 * math.pi / LON)
    stacked = np.concatenate([np.cos(angles), -np.sin(angles)], axis=0) / math.sqrt(LON)
    return jnp.asarray(stacked.astype(np.float32)).astype(jnp.bfloat16)


def double_orders(table):
    order = np.arange(2 * ORDERS) % ORDERS
    factor = np.where(order == 0, 1.0, 2.0).astype(np.float32)
    return (table.astype(jnp.float32) * factor[:, None]).astype(jnp.bfloat16)


def dot32(expression, left, right):
    return jnp.einsum(expression, left, right, preferred_element_type=jnp.float32).astype(jnp.bfloat16)


def rows_per_step(rows, most):
    return max(d for d in range(1, most + 1) if rows % d == 0)


def dot_f32(left, right, contract):
    return lax.dot_general(left, right, (contract, ((), ())), preferred_element_type=jnp.float32)


def store_orders(out_ref, row, value):
    polar, _, mine, _ = out_ref.shape
    for p in range(polar):
        out_ref[p, row] = value[p * mine:(p + 1) * mine]


def load_orders(in_ref, row):
    polar, _, mine, width = in_ref.shape
    return in_ref[:, row].reshape(polar * mine, width)


def call_rows(body, inputs, row_axes, out_shape, out_axis, step, flops):
    def block(shape, axis):
        if axis is None:
            return pl.BlockSpec(shape, lambda i: (0,) * len(shape))
        sizes = tuple(step if d == axis else s for d, s in enumerate(shape))
        return pl.BlockSpec(sizes, lambda i: tuple(i if d == axis else 0 for d in range(len(shape))))

    moved = sum(2 * math.prod(x.shape) for x in inputs) + 2 * math.prod(out_shape)
    return pl.pallas_call(
        body,
        grid=(out_shape[out_axis] // step,),
        in_specs=[block(x.shape, axis) for x, axis in zip(inputs, row_axes)],
        out_specs=block(out_shape, out_axis),
        out_shape=jax.ShapeDtypeStruct(out_shape, jnp.bfloat16),
        compiler_params=pltpu.CompilerParams(vmem_limit_bytes=VMEM_BYTES),
        cost_estimate=pl.CostEstimate(flops=flops, bytes_accessed=moved, transcendentals=0),
    )(*inputs)


def field_to_orders(cube, table, polar):
    lat, lon, chan = cube.shape

    def body(x_ref, table_ref, out_ref):
        def one(i, carry):
            y = dot_f32(table_ref[...], x_ref[i], ((1,), (0,)))
            both = jnp.concatenate([y[:ORDERS], y[ORDERS:]], axis=1)
            store_orders(out_ref, i, both.astype(jnp.bfloat16))
            return carry

        lax.fori_loop(0, x_ref.shape[0], one, 0)

    shape = (polar, lat, ORDERS // polar, 2 * chan)
    return call_rows(body, (cube, table), (0, None), shape, 1, rows_per_step(lat, 10),
                     4 * lat * lon * chan * ORDERS)


def orders_to_field(orders, table):
    polar, lat, mine, width = orders.shape
    lon, chan = table.shape[0], width // 2

    def body(g_ref, table_ref, out_ref):
        def one(i, carry):
            g = load_orders(g_ref, i)
            y = dot_f32(table_ref[:, :ORDERS], g[:, :chan], ((1,), (0,)))
            y += dot_f32(table_ref[:, ORDERS:], g[:, chan:], ((1,), (0,)))
            out_ref[i] = y.astype(jnp.bfloat16)
            return carry

        lax.fori_loop(0, out_ref.shape[0], one, 0)

    return call_rows(body, (orders, table), (1, None), (lat, lon, chan), 0, rows_per_step(lat, 10),
                     4 * lat * lon * chan * ORDERS)


def channels_to_orders(field, table, polar):
    lat, chan, lon = field.shape

    def body(x_ref, table_ref, out_ref):
        rows = x_ref.shape[0]
        x = x_ref[...].reshape(rows * chan, lon)
        y = dot_f32(table_ref[...], x, ((1,), (1,)))
        for i in range(rows):
            part = y[:, i * chan:(i + 1) * chan]
            both = jnp.concatenate([part[:ORDERS], part[ORDERS:]], axis=1)
            store_orders(out_ref, i, both.astype(jnp.bfloat16))

    shape = (polar, lat, ORDERS // polar, 2 * chan)
    return call_rows(body, (field, table), (0, None), shape, 1, rows_per_step(lat, 5),
                     4 * lat * lon * chan * ORDERS)


def orders_to_channels(orders, table):
    polar, lat, mine, width = orders.shape
    lon, chan = table.shape[1], width // 2

    def body(g_ref, table_ref, out_ref):
        rows = out_ref.shape[0]
        parts = [load_orders(g_ref, i).astype(jnp.float32) for i in range(rows)]
        real = jnp.concatenate([g[:, :chan] for g in parts], axis=1)
        imag = jnp.concatenate([g[:, chan:] for g in parts], axis=1)
        both = jnp.concatenate([real, imag], axis=0).astype(jnp.bfloat16)
        y = dot_f32(both, table_ref[...], ((0,), (0,)))
        out_ref[...] = y.astype(jnp.bfloat16).reshape(rows, chan, lon)

    return call_rows(body, (orders, table), (1, None), (lat, chan, lon), 0, rows_per_step(lat, 5),
                     4 * lat * lon * chan * ORDERS)


def exchange(blocks, axis):
    return lax.all_to_all(blocks, axis, split_axis=0, concat_axis=0, tiled=True)


def on_device(grid_input, cotangent, forward_legendre, inverse_legendre, filter_weight):
    azimuth = lax.axis_size("azimuth")
    polar = lax.axis_size("polar")
    plain = host_table()
    doubled = double_orders(plain)
    lat = grid_input.shape[0]
    lon = grid_input.shape[1] // C
    chan = cotangent.shape[1]
    total_lat, orders, degrees = forward_legendre.shape
    mine = orders // azimuth
    depth = degrees // polar
    local = lax.dynamic_slice_in_dim(plain, lax.axis_index("azimuth") * lon, lon, 1)

    spectrum = exchange(field_to_orders(grid_input.reshape(lat, lon, C), local, polar), "polar")
    grad_synthesis = exchange(channels_to_orders(cotangent, doubled, polar), "polar")

    weight = filter_weight.reshape(depth, 2, C, C)
    upper = jnp.concatenate([weight[:, 0], weight[:, 1]], axis=2)
    lower = jnp.concatenate([-weight[:, 1], weight[:, 0]], axis=2)
    kernel = jnp.concatenate([upper, lower], axis=1)

    grad_mixed = dot32(
        "amk,aml->mkl", grad_synthesis.reshape(total_lat, orders, 2 * chan), inverse_legendre
    )
    grad_mixed = exchange(grad_mixed, "azimuth").reshape(azimuth, mine, 2, chan, degrees)
    grad_mixed = grad_mixed.transpose(4, 1, 2, 0, 3).reshape(degrees, mine, 2 * C)
    grad_mixed = exchange(grad_mixed, "polar").reshape(polar, depth, mine, 2 * C)
    grad_modes = dot32("slmj,lkj->slmk", grad_mixed, kernel)
    grad_modes = exchange(grad_modes, "polar").reshape(degrees, mine, 2 * C)
    grad_modes = lax.all_gather(grad_modes.transpose(1, 0, 2), "azimuth", axis=0, tiled=True)

    coefficients = dot32(
        "amk,aml->mkl", spectrum.reshape(total_lat, orders, 2 * C), forward_legendre
    )
    coefficients = lax.psum_scatter(coefficients, "azimuth", scatter_dimension=0, tiled=True)
    coefficients = exchange(coefficients.transpose(2, 0, 1), "polar")
    mixed = dot32("slmk,lkj->slmj", coefficients.reshape(polar, depth, mine, 2 * C), kernel)
    mixed = exchange(mixed, "polar").reshape(degrees, mine, 2, azimuth, chan)
    mixed = mixed.transpose(3, 1, 0, 2, 4).reshape(orders, degrees, 2 * chan)
    mixed = exchange(mixed, "azimuth")

    grad_rows = dot32("mlk,aml->amk", grad_modes, forward_legendre)
    grad_rows = exchange(grad_rows.reshape(polar, lat, orders, 2 * C), "polar")
    rows = dot32("mlk,aml->amk", mixed, inverse_legendre)
    rows = exchange(rows.reshape(polar, lat, orders, 2 * chan), "polar")
    filtered = orders_to_channels(rows, doubled)
    grid_grad = orders_to_field(grad_rows, local.T)
    return filtered, grid_grad.reshape(lat, lon * C)


def solution(mesh):
    return jax.shard_map(
        on_device,
        mesh=mesh,
        in_specs=(
            P("polar", "azimuth"),
            P("polar", "azimuth", None),
            P(None, "polar", None),
            P(None, "polar", None),
            P("polar", None),
        ),
        out_specs=(P("polar", "azimuth", None), P("polar", "azimuth")),
        check_vma=False,
    )
```

time: 1630 us -> 1050 us (0.64); the launches traced: 1610 us -> 1050 us
  local copies, waits for them, and re-layouts: 724 us -> 106 us
  blocking collectives: 0 us -> 387 us
  waiting for transfers between devices: 613 us -> 257 us
  Pallas kernels: 0 us -> 106 us
  starting transfers between devices: 68.3 us -> 18.3 us
  other arithmetic: 28.5 us -> 3.92 us
  matrix products: 174 us -> 155 us
    all_to_all x14 -> x4, waiting for transfers between devices: 613 us -> 183 us  [exchange(): return lax.all_to_all(blocks, axis, split_axis=0, concat_axis=0, tiled=True)]
    all_to_all x0 -> x6, blocking collectives: none -> 387 us  [exchange(): return lax.all_to_all(blocks, axis, split_axis=0, concat_axis=0, tiled=True)]
    all_to_all x20 -> x0, local copies, waits for them, and re-layouts: 296 us -> none  [the longest x2 62.4 us: on_device(): lax.all_to_all(grad_full, 'azimuth', split_axis=1, concat_axis=2, tiled=T...]
    unnamed x33 -> x4, local copies, waits for them, and re-layouts: 191 us -> 2.32 us
    pallas_call x0 -> x4, Pallas kernels: none -> 106 us  [call_rows(): pl.pallas_call(body, grid=(out_shape[out_axis] // step,), in_specs=[block...]
    all_gather x0 -> x1, waiting for transfers between devices: none -> 73.4 us  [on_device(): lax.all_gather(grad_modes.transpose(1, 0, 2), 'azimuth', axis=0, tiled=True)]
    convert_element_type x9 -> x4, local copies, waits for them, and re-layouts: 101 us -> 32.2 us  [dot32(): jnp.einsum(expression, left, right, preferred_element_type=jnp.float32)]
    reshape x10 -> x6, local copies, waits for them, and re-layouts: 108 us -> 56.7 us  [the longest x1 21.2 us: on_device(): return (filtered, grid_grad.reshape(lat, lon * C))]
  transfers between devices with their start and end apart: 14 -> 6, of which waited for: 5 -> 4; matrix products, arithmetic and copies ran while one was open for 48% -> 16% of each run, Pallas kernels for 0% -> 5%
where the time goes in v1:
time: 1050 us
  blocking collectives  387 us (37%)
  waiting for transfers between devices  257 us (24%)
  matrix products  155 us (15%)
  local copies, waits for them, and re-layouts  106 us (10%)
  Pallas kernels  106 us (10%)
  starting transfers between devices  18.3 us (2%)
  between operations  14.4 us (1%)
    all_to_all x6, blocking collectives, exchange(): return lax.all_to_all(blocks, axis, split_axis=0, concat_axis=0, tiled=True)  387 us
    all_to_all x4, waiting for transfers between devices, exchange(): return lax.all_to_all(blocks, axis, split_axis=0, concat_axis=0, tiled=True)  183 us
    dot_general x6, matrix products, dot32(): jnp.einsum(expression, left, right, preferred_element_type=jnp.float32)  155 us
    pallas_call x4, Pallas kernels, call_rows(): pl.pallas_call(body, grid=(out_shape[out_axis] // step,), in_specs=[block...  106 us
    all_gather x1, waiting for transfers between devices, on_device(): lax.all_gather(grad_modes.transpose(1, 0, 2), 'azimuth', axis=0, tiled=True)  73.4 us
    convert_element_type x4, local copies, waits for them, and re-layouts, dot32(): jnp.einsum(expression, left, right, preferred_element_type=jnp.float32)  32.2 us
    reshape x1, local copies, waits for them, and re-layouts, on_device(): return (filtered, grid_grad.reshape(lat, lon * C))  21.2 us
  transfers between devices with their start and end apart: 6, of which 4 were waited for; matrix products, arithmetic and copies ran while one was open for 16% of the time, Pallas kernels for 5%

profile of v1, /device:TPU:0, one launch (start us, length us, event | category | flops | bytes accessed | tf_op | source)
XLA Modules:
  0.0 1047.7 jit_solution(8948330401723549560)
XLA Ops:
  7.2 0.0 reduce-scatter.2.cloned.1.call-start
  7.2 19.0 %reshape.47.x_ref = bf16[90,360,192]{2,1,0:T(8,128)(2,1)} reshape(bf16[90,69120]{1,0:T(8,128)(2,1)} %param.7) | data formatting | bytes 24883200 | tf_op jit(solution)/shard_map/reshape | solution.py:159
  26.2 1.0 dynamic-slice_bitcast_fusion
  27.3 0.2 copy.41.table_ref
  27.5 35.5 %shard_map.86 = bf16[8,90,32,384]{3,2,1,0:T(8,128)(2,1)} custom-call(bf16[90,360,192]{2,1,0:T(8,128)(2,1)} %reshape.47.x_ref, bf16[512,360]{1,0:T(8,128)(2,1)S(1)} %copy.41.table_ref), custom_call_target="tpu_custom_call" | custom-call | flops 6370099200 | bytes 30504960 | tf_op jit(solution)/shard_map/pallas_call | solution.py:62
  63.0 202.3 %all_to_all.50 = bf16[8,90,32,384]{3,2,1,0:T(8,128)(2,1)} all-to-all(bf16[8,90,32,384]{3,2,1,0:T(8,128)(2,1)} %shard_map.86), channel_id=1, replica_groups=mesh['polar'=8,'azimuth'=4] {'polar'}, dimensions={0} | all-to-all | bytes 35389440 | tf_op jit(solution)/shard_map/all_to_all | solution.py:143
  265.3 70.6 %fusion.14 = bf16[32,384,256]{2,1,0:T(8,128)(2,1)} fusion(bf16[720,32,256]{2,1,0:T(8,128)(2,1)} %param.9, bf16[720,32,384]{2,1,0:T(8,128)(2,1)} %bitcast.56), kind=kOutput, calls=%fused_computation.15 | convolution fusion | flops 4532994048 | bytes 35782656 | tf_op jit(solution)/shard_map/amk,aml->mkl/dot_general | solution.py:32
  335.9 0.0 reduce-scatter.2.cloned.1.call-update
  335.9 1.4 copy-done
  337.3 19.6 %shard_map.88 = bf16[8,90,32,96]{3,2,1,0:T(8,128)(2,1)} custom-call(bf16[90,48,1440]{2,1,0:T(8,128)(2,1)} %x_ref.1, bf16[512,1440]{1,0:T(8,128)(2,1)S(1)} %copy-done), custom_call_target="tpu_custom_call" | custom-call | flops 6370099200 | bytes 18339840 | tf_op jit(solution)/shard_map/pallas_call | solution.py:62
  356.9 72.5 %all_to_all.51 = bf16[8,90,32,96]{3,2,1,0:T(8,128)(2,1)} all-to-all(bf16[8,90,32,96]{3,2,1,0:T(8,128)(2,1)} %shard_map.88), channel_id=1, replica_groups=mesh['polar'=8,'azimuth'=4] {'polar'}, dimensions={0} | all-to-all | bytes 8847360 | tf_op jit(solution)/shard_map/all_to_all | solution.py:143
  429.3 22.4 %fusion.23 = bf16[32,96,256]{2,1,0:T(8,128)(2,1)S(1)} fusion(bf16[720,32,256]{2,1,0:T(8,128)(2,1)} %param.10, bf16[720,32,96]{2,1,0:T(8,128)(2,1)} %bitcast.62), kind=kOutput, calls=%fused_computation.20 | convolution fusion | flops 1133248512 | bytes 17793024 | tf_op jit(solution)/shard_map/amk,aml->mkl/dot_general | solution.py:32
  451.7 42.0 %all_to_all.52 = bf16[32,96,256]{2,1,0:T(8,128)(2,1)S(1)} all-to-all(bf16[32,96,256]{2,1,0:T(8,128)(2,1)S(1)} %fusion.23), channel_id=1, replica_groups=mesh['polar'=8,'azimuth'=4] {'azimuth'}, dimensions={0} | all-to-all | bytes 3145728 | tf_op jit(solution)/shard_map/all_to_all | solution.py:143
  493.8 0.1 copy.52
  493.9 2.1 copy.53
  496.1 3.6 all-to-all-start.7
  499.7 0.0 all-gather.2.cloned.1.call-start
  499.7 9.6 reshape.46
  509.3 3.9 fusion.38
  513.2 0.9 copy-done.1
  514.1 3.1 slice_bitcast_fusion
  517.2 3.4 all-to-all-done.7
  520.6 8.3 fusion.30
  528.9 0.2 copy.55
  529.1 23.4 %all_to_all.53 = bf16[8,32,8,384]{3,2,1,0:T(8,128)(2,1)S(1)} all-to-all(bf16[8,32,8,384]{3,2,1,0:T(8,128)(2,1)S(1)} %copy.55), channel_id=1, replica_groups=mesh['polar'=8,'azimuth'=4] {'polar'}, dimensions={0} | all-to-all | bytes 3145728 | tf_op jit(solution)/shard_map/all_to_all | solution.py:143
  552.5 1.4 copy.56
  554.0 0.0 all-gather.2.cloned.1.call-update
  554.0 0.0 reduce-scatter.2.cloned.1.call-done
  554.0 2.2 copy.44
  556.2 23.4 %all_to_all.54 = bf16[256,8,384]{2,1,0:T(8,128)(2,1)S(1)} all-to-all(bf16[256,8,384]{2,1,0:T(8,128)(2,1)S(1)} %copy.44), channel_id=1, replica_groups=mesh['polar'=8,'azimuth'=4] {'polar'}, dimensions={0} | all-to-all | bytes 3145728 | tf_op jit(solution)/shard_map/all_to_all | solution.py:143
  579.6 8.1 fusion.33
  587.7 0.2 copy.46
  587.9 23.4 %all_to_all.55 = bf16[8,32,8,384]{3,2,1,0:T(8,128)(2,1)S(1)} all-to-all(bf16[8,32,8,384]{3,2,1,0:T(8,128)(2,1)S(1)} %copy.46), channel_id=1, replica_groups=mesh['polar'=8,'azimuth'=4] {'polar'}, dimensions={0} | all-to-all | bytes 3145728 | tf_op jit(solution)/shard_map/all_to_all | solution.py:143
  611.3 4.6 reshape.50
  615.9 7.1 copy.47
  622.9 4.0 all-to-all-start.3
  626.9 73.4 %all-gather.2.cloned.1.call-done = bf16[32,256,384]{2,1,0:T(8,128)(2,1)} async-done(((bf16[8,256,384]{2,1,0:T(8,128)(2,1)}), bf16[32,256,384]{2,1,0:T(8,128)(2,1)}) %all-gather.2.cloned.1.call-update) | async-done | bytes 6291472 | tf_op jit(solution)/shard_map/all_gather | solution.py:175
  700.3 25.6 %convert_bitcast_fusion = bf16[720,32,384]{2,0,1:T(8,128)(2,1)} fusion(bf16[32,256,384]{2,1,0:T(8,128)(2,1)} %all-gather.2.cloned.1.call-done, bf16[720,32,256]{2,1,0:T(8,128)(2,1)} %param.9), kind=kOutput, calls=%fused_computation.2 | convolution fusion | flops 4538695680 | bytes 35782656 | tf_op jit(solution)/shard_map/mlk,aml->amk/dot_general | solution.py:32
  725.9 23.4 %copy.58 = bf16[720,32,384]{2,1,0:T(8,128)(2,1)} copy(bf16[720,32,384]{2,0,1:T(8,128)(2,1)} %convert_bitcast_fusion) | data formatting | bytes 35389440 | tf_op jit(solution)/shard_map/convert_element_type | solution.py:32
  749.4 6.0 all-to-all-start.9
  755.4 19.9 %convert_bitcast_fusion.1 = bf16[720,32,96]{0,2,1:T(8,128)(2,1)} fusion(bf16[32,256,96]{1,2,0:T(8,128)(2,1)S(1)} %all-to-all-done.3, bf16[720,32,256]{2,1,0:T(8,128)(2,1)} %param.10), kind=kOutput, calls=%fused_computation.14 | convolution fusion | flops 1134673920 | bytes 17793024 | tf_op jit(solution)/shard_map/mlk,aml->amk/dot_general | solution.py:32
  775.3 8.4 copy.49
  783.7 165.2 %all-to-all-done.9.g_ref = bf16[8,90,32,384]{3,2,1,0:T(8,128)(2,1)} async-done(((bf16[8,90,32,384]{3,2,1,0:T(8,128)(2,1)}), bf16[8,90,32,384]{3,2,1,0:T(8,128)(2,1)}, u32[]{:S(2)}, u32[]{:S(2)}) %all-to-all-start.9) | async-done | bytes 17694752 | tf_op jit(solution)/shard_map/all_to_all | solution.py:143
  949.0 4.7 all-to-all-start.4
  953.7 31.6 %shard_map.89 = bf16[90,360,192]{2,1,0:T(8,128)(2,1)} custom-call(bf16[8,90,32,384]{3,2,1,0:T(8,128)(2,1)} %all-to-all-done.9.g_ref, bf16[360,512]{1,0:T(8,128)(2,1)S(1)} %get-tuple-element.4.table_ref), custom_call_target="tpu_custom_call" | custom-call | flops 6370099200 | bytes 30504960 | tf_op jit(solution)/shard_map/pallas_call | solution.py:62
  985.4 21.2 %reshape.59 = bf16[90,69120]{1,0:T(8,128)(2,1)} reshape(bf16[90,360,192]{2,1,0:T(8,128)(2,1)} %shard_map.89) | data formatting | bytes 24883200 | tf_op jit(solution)/shard_map/reshape | solution.py:193
  1006.6 14.5 %all-to-all-done.4.g_ref = bf16[8,90,32,96]{3,2,1,0:T(8,128)(2,1)} async-done(((bf16[8,90,32,96]{3,2,1,0:T(8,128)(2,1)}), bf16[8,90,32,96]{3,2,1,0:T(8,128)(2,1)}, u32[]{:S(2)}, u32[]{:S(2)}) %all-to-all-start.4) | async-done | bytes 4423712 | tf_op jit(solution)/shard_map/all_to_all | solution.py:143
  1021.1 19.5 %shard_map.87 = bf16[90,48,1440]{2,1,0:T(8,128)(2,1)} custom-call(bf16[8,90,32,96]{3,2,1,0:T(8,128)(2,1)} %all-to-all-done.4.g_ref, bf16[512,1440]{1,0:T(8,128)(2,1)S(1)} %copy-done), custom_call_target="tpu_custom_call" | custom-call | flops 6370099200 | bytes 18339840 | tf_op jit(solution)/shard_map/pallas_call | solution.py:62
  (3 shorter events, 0.0 us)
Async XLA Ops:
  7.2 546.9 %reduce-scatter.2.cloned.1.call-start = ((), (), s32[]{:S(2)}) async-start(), calls=%async_computation.11 | async-start | bytes 7864320 | tf_op jit(solution)/shard_map/reduce_scatter | solution.py:180
  335.9 1.4 copy-start
  496.1 24.5 %all-to-all-start.7 = ((bf16[256,8,384]{2,1,0:T(8,128)(2,1)}), bf16[256,8,384]{2,1,0:T(8,128)(2,1)S(1)}, u32[]{:S(2)}, u32[]{:S(2)}) async-start(bf16[256,8,384]{2,1,0:T(8,128)(2,1)} %copy.53), calls=%async_computation.8 | async-start | bytes 3145728 | tf_op jit(solution)/shard_map/all_to_all | solution.py:143
  499.7 200.6 %all-gather.2.cloned.1.call-start = ((), (), s32[]{:S(2)}) async-start(), calls=%async_computation.12 | async-start | bytes 7864320 | tf_op jit(solution)/shard_map/all_gather | solution.py:175
  509.3 4.9 copy-start.1
  622.9 126.4 %all-to-all-start.3 = ((bf16[32,256,96]{1,2,0:T(8,128)(2,1)}), bf16[32,256,96]{1,2,0:T(8,128)(2,1)S(1)}, u32[]{:S(2)}, u32[]{:S(2)}) async-start(bf16[32,256,96]{1,2,0:T(8,128)(2,1)} %bitcast.61), calls=%async_computation.4 | async-start | bytes 3145728 | tf_op jit(solution)/shard_map/all_to_all | solution.py:143
  749.4 199.6 %all-to-all-start.9 = ((bf16[8,90,32,384]{3,2,1,0:T(8,128)(2,1)}), bf16[8,90,32,384]{3,2,1,0:T(8,128)(2,1)}, u32[]{:S(2)}, u32[]{:S(2)}) async-start(bf16[8,90,32,384]{3,2,1,0:T(8,128)(2,1)} %bitcast.54), calls=%async_computation.10 | async-start | bytes 35389440 | tf_op jit(solution)/shard_map/all_to_all | solution.py:143
  949.0 72.1 %all-to-all-start.4 = ((bf16[8,90,32,96]{3,2,1,0:T(8,128)(2,1)}), bf16[8,90,32,96]{3,2,1,0:T(8,128)(2,1)}, u32[]{:S(2)}, u32[]{:S(2)}) async-start(bf16[8,90,32,96]{3,2,1,0:T(8,128)(2,1)} %bitcast.55), calls=%async_computation.5 | async-start | bytes 11796480 | tf_op jit(solution)/shard_map/all_to_all | solution.py:143
Sparse Core Ops, SparseCore 0:
  336.0 110.8 reduce-scatter.1
  554.1 146.1 all-gather.1

commit v2 on v1

--- a/solution.py
+++ b/solution.py
@@ -137,6 +137,120 @@
 
     return call_rows(body, (orders, table), (1, None), (lat, chan, lon), 0, rows_per_step(lat, 5),
                      4 * lat * lon * chan * ORDERS)
+
+
+def lane_tiles(width):
+    return -(-width // 128)
+
+
+def split_rows(in_ref, wide_ref):
+    rows, block, width = in_ref.shape
+    for j in range(lane_tiles(width)):
+        lanes = min(128, width - 128 * j)
+        part = in_ref[:, :, 128 * j:128 * j + lanes].astype(jnp.float32)
+        wide_ref[j, :rows * block, :lanes] = part.reshape(rows * block, lanes)
+
+
+def order_rows(wide_ref, m, rows, block):
+    parts = [wide_ref[j, pl.ds(m, rows, stride=block), :] for j in range(wide_ref.shape[0])]
+    return jnp.concatenate(parts, axis=1).astype(jnp.bfloat16)
+
+
+def legendre_blocks(table):
+    rows, orders, _ = table.shape
+    block = 16 if orders % 16 == 0 else orders
+    step = max(d for d in range(8, 241, 8) if rows % d == 0)
+    return step, block
+
+
+def analysis(field, table, degrees_first):
+    rows, orders, width = field.shape
+    degrees = table.shape[2]
+    step, block = legendre_blocks(table)
+    shape = (degrees, width) if degrees_first else (width, degrees)
+
+    def body(s_ref, f_ref, out_ref, s_wide, f_wide, total):
+        split_rows(s_ref, s_wide)
+        split_rows(f_ref, f_wide)
+
+        @pl.when(pl.program_id(1) == 0)
+        def _():
+            total[...] = jnp.zeros_like(total)
+
+        for m in range(block):
+            s = order_rows(s_wide, m, step, block)[:, :width]
+            f = order_rows(f_wide, m, step, block)
+            pair = (f, s) if degrees_first else (s, f)
+            total[m] += dot_f32(*pair, ((0,), (0,)))
+
+        @pl.when(pl.program_id(1) == pl.num_programs(1) - 1)
+        def _():
+            out_ref[...] = total[...].astype(jnp.bfloat16)
+
+    return pl.pallas_call(
+        body,
+        grid=(orders // block, rows // step),
+        in_specs=[
+            pl.BlockSpec((step, block, width), lambda i, j: (j, i, 0)),
+            pl.BlockSpec((step, block, degrees), lambda i, j: (j, i, 0)),
+        ],
+        out_specs=pl.BlockSpec((block, *shape), lambda i, j: (i, 0, 0)),
+        out_shape=jax.ShapeDtypeStruct((orders, *shape), jnp.bfloat16),
+        scratch_shapes=[
+            pltpu.VMEM((lane_tiles(width), (step + 1) * block, 128), jnp.float32),
+            pltpu.VMEM((lane_tiles(degrees), (step + 1) * block, 128), jnp.float32),
+            pltpu.VMEM((block, *shape), jnp.float32),
+        ],
+        compiler_params=pltpu.CompilerParams(vmem_limit_bytes=VMEM_BYTES),
+        cost_estimate=pl.CostEstimate(
+            flops=2 * rows * orders * width * degrees,
+            bytes_accessed=2 * rows * orders * (width + degrees),
+            transcendentals=0,
+        ),
+    )(field, table)
+
+
+def synthesis(modes, table):
+    orders, degrees, width = modes.shape
+    rows = table.shape[0]
+    step, block = legendre_blocks(table)
+    tiles = lane_tiles(width)
+
+    def body(g_ref, f_ref, out_ref, f_wide, out_wide):
+        split_rows(f_ref, f_wide)
+        for m in range(block):
+            f = order_rows(f_wide, m, step, block)
+            y = dot_f32(f, g_ref[m], ((1,), (0,)))
+            if width % 128:
+                fill = jnp.zeros((step, 128 * tiles - width), jnp.float32)
+                y = jnp.concatenate([y, fill], axis=1)
+            for j in range(tiles):
+                out_wide[j, pl.ds(m, step, stride=block), :] = y[:, 128 * j:128 * (j + 1)]
+        for j in range(tiles):
+            lanes = min(128, width - 128 * j)
+            part = out_wide[j, :step * block].reshape(step, block, 128)[:, :, :lanes]
+            out_ref[:, :, 128 * j:128 * j + lanes] = part.astype(jnp.bfloat16)
+
+    return pl.pallas_call(
+        body,
+        grid=(orders // block, rows // step),
+        in_specs=[
+            pl.BlockSpec((block, degrees, width), lambda i, j: (i, 0, 0)),
+            pl.BlockSpec((step, block, degrees), lambda i, j: (j, i, 0)),
+        ],
+        out_specs=pl.BlockSpec((step, block, width), lambda i, j: (j, i, 0)),
+        out_shape=jax.ShapeDtypeStruct((rows, orders, width), jnp.bfloat16),
+        scratch_shapes=[
+            pltpu.VMEM((lane_tiles(degrees), (step + 1) * block, 128), jnp.float32),
+            pltpu.VMEM((tiles, (step + 1) * block, 128), jnp.float32),
+        ],
+        compiler_params=pltpu.CompilerParams(vmem_limit_bytes=VMEM_BYTES),
+        cost_estimate=pl.CostEstimate(
+            flops=2 * rows * orders * width * degrees,
+            bytes_accessed=2 * rows * orders * (width + degrees),
+            transcendentals=0,
+        ),
+    )(modes, table)
 
 
 def exchange(blocks, axis):
@@ -156,37 +270,39 @@
     depth = degrees // polar
     local = lax.dynamic_slice_in_dim(plain, lax.axis_index("azimuth") * lon, lon, 1)
 
-    spectrum = exchange(field_to_orders(grid_input.reshape(lat, lon, C), local, polar), "polar")
     grad_synthesis = exchange(channels_to_orders(cotangent, doubled, polar), "polar")
+    spectrum = field_to_orders(grid_input.reshape(lat, lon, C), local, polar)
+
+    grad_synthesis, spectrum = lax.optimization_barrier((grad_synthesis, spectrum))
 
     weight = filter_weight.reshape(depth, 2, C, C)
     upper = jnp.concatenate([weight[:, 0], weight[:, 1]], axis=2)
     lower = jnp.concatenate([-weight[:, 1], weight[:, 0]], axis=2)
     kernel = jnp.concatenate([upper, lower], axis=1)
 
-    grad_mixed = dot32(
-        "amk,aml->mkl", grad_synthesis.reshape(total_lat, orders, 2 * chan), inverse_legendre
+    grad_mixed = analysis(
+        grad_synthesis.reshape(total_lat, orders, 2 * chan), inverse_legendre, False
     )
     grad_mixed = exchange(grad_mixed, "azimuth").reshape(azimuth, mine, 2, chan, degrees)
     grad_mixed = grad_mixed.transpose(4, 1, 2, 0, 3).reshape(degrees, mine, 2 * C)
     grad_mixed = exchange(grad_mixed, "polar").reshape(polar, depth, mine, 2 * C)
     grad_modes = dot32("slmj,lkj->slmk", grad_mixed, kernel)
     grad_modes = exchange(grad_modes, "polar").reshape(degrees, mine, 2 * C)
-    grad_modes = lax.all_gather(grad_modes.transpose(1, 0, 2), "azimuth", axis=0, tiled=True)
-
-    coefficients = dot32(
-        "amk,aml->mkl", spectrum.reshape(total_lat, orders, 2 * C), forward_legendre
-    )
+    grad_modes, spectrum = lax.optimization_barrier((grad_modes.transpose(1, 0, 2), spectrum))
+    grad_modes = lax.all_gather(grad_modes, "azimuth", axis=0, tiled=True)
+
+    spectrum = exchange(spectrum, "polar").reshape(total_lat, orders, 2 * C)
+    coefficients = analysis(spectrum, forward_legendre, True)
+    coefficients, grad_modes = lax.optimization_barrier((coefficients, grad_modes))
     coefficients = lax.psum_scatter(coefficients, "azimuth", scatter_dimension=0, tiled=True)
-    coefficients = exchange(coefficients.transpose(2, 0, 1), "polar")
+    grad_rows = synthesis(grad_modes, forward_legendre)
+    grad_rows = exchange(grad_rows.reshape(polar, lat, orders, 2 * C), "polar")
+
+    coefficients = exchange(coefficients.transpose(1, 0, 2), "polar")
     mixed = dot32("slmk,lkj->slmj", coefficients.reshape(polar, depth, mine, 2 * C), kernel)
     mixed = exchange(mixed, "polar").reshape(degrees, mine, 2, azimuth, chan)
     mixed = mixed.transpose(3, 1, 0, 2, 4).reshape(orders, degrees, 2 * chan)
-    mixed = exchange(mixed, "azimuth")
-
-    grad_rows = dot32("mlk,aml->amk", grad_modes, forward_legendre)
-    grad_rows = exchange(grad_rows.reshape(polar, lat, orders, 2 * C), "polar")
-    rows = dot32("mlk,aml->amk", mixed, inverse_legendre)
+    rows = synthesis(exchange(mixed, "azimuth"), inverse_legendre)
     rows = exchange(rows.reshape(polar, lat, orders, 2 * chan), "polar")
     filtered = orders_to_channels(rows, doubled)
     grid_grad = orders_to_field(grad_rows, local.T)

time: 1050 us -> 979 us (0.932)
  blocking collectives: 387 us -> 111 us
  waiting for transfers between devices: 257 us -> 515 us
  matrix products: 155 us -> 13.5 us
  Pallas kernels: 106 us -> 210 us
  local copies, waits for them, and re-layouts: 106 us -> 79.5 us
  starting transfers between devices: 18.3 us -> 31 us
    all_to_all x6 -> x4, blocking collectives: 387 us -> 111 us  [exchange(): return lax.all_to_all(blocks, axis, split_axis=0, concat_axis=0, tiled=True)]
    all_to_all x4 -> x6, waiting for transfers between devices: 183 us -> 406 us  [exchange(): return lax.all_to_all(blocks, axis, split_axis=0, concat_axis=0, tiled=True)]
    dot_general x6 -> x2, matrix products: 155 us -> 13.5 us  [dot32(): jnp.einsum(expression, left, right, preferred_element_type=jnp.float32)]
    reduce_scatter x1, waiting for transfers between devices: 0.02 us -> 108 us  [on_device(): lax.psum_scatter(coefficients, 'azimuth', scatter_dimension=0, tiled=True)]
    pallas_call x0 -> x4, Pallas kernels: none -> 104 us  [the longest x2 59.1 us: analysis(): pl.pallas_call(body, grid=(orders // block, rows // step), in_specs=[pl.B...]
    all_gather x1, waiting for transfers between devices: 73.4 us -> 0.01 us  [on_device(): grad_modes = lax.all_gather(grad_modes, 'azimuth', axis=0, tiled=True)]
    convert_element_type x4 -> x2, local copies, waits for them, and re-layouts: 32.2 us -> 0.34 us  [dot32(): jnp.einsum(expression, left, right, preferred_element_type=jnp.float32)]
    all_to_all x4 -> x6, starting transfers between devices: 18.3 us -> 30.9 us  [exchange(): return lax.all_to_all(blocks, axis, split_axis=0, concat_axis=0, tiled=True)]
  transfers between devices with their start and end apart: 6 -> 8, of which waited for: 4 -> 7; matrix products, arithmetic and copies ran while one was open for 16% -> 6% of each run, Pallas kernels for 5% -> 16%
where the time goes in v2:
time: 979 us; the launch traced here: 976 us
  waiting for transfers between devices  515 us (53%)
  Pallas kernels  210 us (21%)
  blocking collectives  111 us (11%)
  local copies, waits for them, and re-layouts  79.5 us (8%)
  starting transfers between devices  31 us (3%)
  between operations  14.2 us (1%)
  matrix products  13.5 us (1%)
    all_to_all x6, waiting for transfers between devices, exchange(): return lax.all_to_all(blocks, axis, split_axis=0, concat_axis=0, tiled=True)  406 us
    all_to_all x4, blocking collectives, exchange(): return lax.all_to_all(blocks, axis, split_axis=0, concat_axis=0, tiled=True)  111 us
    reduce_scatter x1, waiting for transfers between devices, on_device(): lax.psum_scatter(coefficients, 'azimuth', scatter_dimension=0, tiled=True)  108 us
    pallas_call x4, Pallas kernels, call_rows(): pl.pallas_call(body, grid=(out_shape[out_axis] // step,), in_specs=[block...  106 us
    pallas_call x2, Pallas kernels, analysis(): pl.pallas_call(body, grid=(orders // block, rows // step), in_specs=[pl.B...  59.1 us
    pallas_call x2, Pallas kernels, synthesis(): pl.pallas_call(body, grid=(orders // block, rows // step), in_specs=[pl.B...  45.1 us
    all_to_all x6, starting transfers between devices, exchange(): return lax.all_to_all(blocks, axis, split_axis=0, concat_axis=0, tiled=True)  30.9 us
    reshape x1, local copies, waits for them, and re-layouts, on_device(): return (filtered, grid_grad.reshape(lat, lon * C))  21.4 us
  transfers between devices with their start and end apart: 8, of which 7 were waited for; matrix products, arithmetic and copies ran while one was open for 6% of the time, Pallas kernels for 16%

profile of v2, /device:TPU:0, one launch (start us, length us, event | category | flops | bytes accessed | tf_op | source)
XLA Modules:
  0.0 976.0 jit_solution(15043851059689444501)
XLA Ops:
  7.2 1.4 copy-done
  8.6 19.3 %shard_map.86 = bf16[8,90,32,96]{3,2,1,0:T(8,128)(2,1)} custom-call(bf16[90,48,1440]{2,1,0:T(8,128)(2,1)} %x_ref.1, bf16[512,1440]{1,0:T(8,128)(2,1)S(1)} %copy-done), custom_call_target="tpu_custom_call" | custom-call | flops 6370099200 | bytes 18339840 | tf_op jit(solution)/shard_map/pallas_call | solution.py:62
  27.9 5.2 all-to-all-start
  33.0 1.0 dynamic-slice_bitcast_fusion
  34.1 0.2 copy.37.table_ref
  34.3 19.0 %reshape.47.x_ref = bf16[90,360,192]{2,1,0:T(8,128)(2,1)} reshape(bf16[90,69120]{1,0:T(8,128)(2,1)} %param.7) | data formatting | bytes 24883200 | tf_op jit(solution)/shard_map/reshape | solution.py:274
  53.3 35.5 %shard_map.87 = bf16[8,90,32,384]{3,2,1,0:T(8,128)(2,1)} custom-call(bf16[90,360,192]{2,1,0:T(8,128)(2,1)} %reshape.47.x_ref, bf16[512,360]{1,0:T(8,128)(2,1)S(1)} %copy.37.table_ref), custom_call_target="tpu_custom_call" | custom-call | flops 6370099200 | bytes 30504960 | tf_op jit(solution)/shard_map/pallas_call | solution.py:62
  88.8 11.8 %all-to-all-done = bf16[8,90,32,96]{3,2,1,0:T(8,128)(2,1)} async-done(((bf16[8,90,32,96]{3,2,1,0:T(8,128)(2,1)}), bf16[8,90,32,96]{3,2,1,0:T(8,128)(2,1)}, u32[]{:S(2)}, u32[]{:S(2)}) %all-to-all-start) | async-done | bytes 4423712 | tf_op jit(solution)/shard_map/all_to_all | solution.py:257
  100.7 16.0 %shard_map.88 = bf16[32,96,256]{2,1,0:T(8,128)(2,1)S(1)} custom-call(bf16[720,32,96]{2,1,0:T(8,128)(2,1)} %bitcast.5.s_ref, bf16[720,32,256]{2,1,0:T(8,128)(2,1)} %f_ref.6), custom_call_target="tpu_custom_call" | custom-call | flops 1132462080 | bytes 16220160 | tf_op jit(solution)/shard_map/pallas_call | solution.py:190
  116.7 39.5 %all_to_all.50 = bf16[32,96,256]{2,1,0:T(8,128)(2,1)S(1)} all-to-all(bf16[32,96,256]{2,1,0:T(8,128)(2,1)S(1)} %shard_map.88), channel_id=1, replica_groups=mesh['polar'=8,'azimuth'=4] {'azimuth'}, dimensions={0} | all-to-all | bytes 3145728 | tf_op jit(solution)/shard_map/all_to_all | solution.py:257
  156.2 0.1 copy.38
  156.3 2.1 copy.39
  158.4 5.0 all-to-all-start.2
  163.4 9.6 reshape.46
  172.9 2.2 fusion.14
  175.2 1.5 copy-done.2
  176.7 3.1 slice_bitcast_fusion
  179.7 4.7 all-to-all-done.2
  184.5 8.1 fusion.9
  192.6 0.2 copy.41
  192.8 23.4 %all_to_all.51 = bf16[8,32,8,384]{3,2,1,0:T(8,128)(2,1)S(1)} all-to-all(bf16[8,32,8,384]{3,2,1,0:T(8,128)(2,1)S(1)} %copy.41), channel_id=1, replica_groups=mesh['polar'=8,'azimuth'=4] {'polar'}, dimensions={0} | all-to-all | bytes 3145728 | tf_op jit(solution)/shard_map/all_to_all | solution.py:257
  216.2 1.4 copy.60
  217.5 6.0 all-to-all-start.4
  223.5 0.0 all-gather.2.cloned.1.call-start
  223.6 0.7 all-gather.2.cloned.1.call-update
  224.3 193.0 %all-to-all-done.4 = bf16[8,90,32,384]{3,2,1,0:T(8,128)(2,1)} async-done(((bf16[8,90,32,384]{3,2,1,0:T(8,128)(2,1)}), bf16[8,90,32,384]{3,2,1,0:T(8,128)(2,1)}, u32[]{:S(2)}, u32[]{:S(2)}) %all-to-all-start.4) | async-done | bytes 17694752 | tf_op jit(solution)/shard_map/all_to_all | solution.py:257
  417.3 43.0 %shard_map.89 = bf16[32,256,384]{2,1,0:T(8,128)(2,1)} custom-call(bf16[720,32,384]{2,1,0:T(8,128)(2,1)} %bitcast.13.s_ref, bf16[720,32,256]{2,1,0:T(8,128)(2,1)} %f_ref.7), custom_call_target="tpu_custom_call" | custom-call | flops 4529848320 | bytes 29491200 | tf_op jit(solution)/shard_map/pallas_call | solution.py:190
  460.3 108.2 %reduce-scatter.2.cloned.1.call-done = bf16[8,256,384]{2,1,0:T(8,128)(2,1)} async-done(((bf16[32,256,384]{2,1,0:T(8,128)(2,1)}), bf16[8,256,384]{2,1,0:T(8,128)(2,1)}) %reduce-scatter.2.cloned.1.call-update) | async-done | bytes 1572880 | tf_op jit(solution)/shard_map/reduce_scatter | solution.py:297
  568.5 2.5 copy.43
  571.0 24.4 %all_to_all.52 = bf16[256,8,384]{2,1,0:T(8,128)(2,1)S(1)} all-to-all(bf16[256,8,384]{2,1,0:T(8,128)(2,1)S(1)} %copy.43), channel_id=1, replica_groups=mesh['polar'=8,'azimuth'=4] {'polar'}, dimensions={0} | all-to-all | bytes 3145728 | tf_op jit(solution)/shard_map/all_to_all | solution.py:257
  595.4 5.5 fusion.6
  600.9 0.2 copy.45
  601.1 23.4 %all_to_all.53 = bf16[8,32,8,384]{3,2,1,0:T(8,128)(2,1)S(1)} all-to-all(bf16[8,32,8,384]{3,2,1,0:T(8,128)(2,1)S(1)} %copy.45), channel_id=1, replica_groups=mesh['polar'=8,'azimuth'=4] {'polar'}, dimensions={0} | all-to-all | bytes 3145728 | tf_op jit(solution)/shard_map/all_to_all | solution.py:257
  624.5 4.6 reshape.55
  629.1 7.1 copy.46
  636.1 4.2 all-to-all-start.7
  640.3 29.8 %shard_map.92 = bf16[720,32,384]{2,1,0:T(8,128)(2,1)} custom-call(bf16[32,256,384]{2,1,0:T(8,128)(2,1)} %all-gather.2.cloned.1.call-done.g_ref, bf16[720,32,256]{2,1,0:T(8,128)(2,1)} %f_ref.7), custom_call_target="tpu_custom_call" | custom-call | flops 4529848320 | bytes 29491200 | tf_op jit(solution)/shard_map/pallas_call | solution.py:234
  670.1 6.6 all-to-all-done.7
  676.8 1.1 copy-done.3
  677.9 5.8 all-to-all-start.9
  683.7 3.1 copy.47.g_ref
  686.9 15.3 %shard_map.90 = bf16[720,32,96]{2,1,0:T(8,128)(2,1)} custom-call(bf16[32,256,96]{2,1,0:T(8,128)(2,1)S(1)} %copy.47.g_ref, bf16[720,32,256]{2,1,0:T(8,128)(2,1)} %f_ref.6), custom_call_target="tpu_custom_call" | custom-call | flops 1132462080 | bytes 16220160 | tf_op jit(solution)/shard_map/pallas_call | solution.py:234
  702.2 175.3 %all-to-all-done.9.g_ref = bf16[8,90,32,384]{3,2,1,0:T(8,128)(2,1)} async-done(((bf16[8,90,32,384]{3,2,1,0:T(8,128)(2,1)}), bf16[8,90,32,384]{3,2,1,0:T(8,128)(2,1)}, u32[]{:S(2)}, u32[]{:S(2)}) %all-to-all-start.9) | async-done | bytes 17694752 | tf_op jit(solution)/shard_map/all_to_all | solution.py:257
  877.5 4.7 all-to-all-start.8
  882.3 31.6 %shard_map.93 = bf16[90,360,192]{2,1,0:T(8,128)(2,1)} custom-call(bf16[8,90,32,384]{3,2,1,0:T(8,128)(2,1)} %all-to-all-done.9.g_ref, bf16[360,512]{1,0:T(8,128)(2,1)S(1)} %get-tuple-element.16.table_ref), custom_call_target="tpu_custom_call" | custom-call | flops 6370099200 | bytes 30504960 | tf_op jit(solution)/shard_map/pallas_call | solution.py:62
  913.9 21.4 %reshape.59 = bf16[90,69120]{1,0:T(8,128)(2,1)} reshape(bf16[90,360,192]{2,1,0:T(8,128)(2,1)} %shard_map.93) | data formatting | bytes 24883200 | tf_op jit(solution)/shard_map/reshape | solution.py:309
  935.3 14.4 %all-to-all-done.8.g_ref = bf16[8,90,32,96]{3,2,1,0:T(8,128)(2,1)} async-done(((bf16[8,90,32,96]{3,2,1,0:T(8,128)(2,1)}), bf16[8,90,32,96]{3,2,1,0:T(8,128)(2,1)}, u32[]{:S(2)}, u32[]{:S(2)}) %all-to-all-start.8) | async-done | bytes 4423712 | tf_op jit(solution)/shard_map/all_to_all | solution.py:257
  949.7 19.5 %shard_map.91 = bf16[90,48,1440]{2,1,0:T(8,128)(2,1)} custom-call(bf16[8,90,32,96]{3,2,1,0:T(8,128)(2,1)} %all-to-all-done.8.g_ref, bf16[512,1440]{1,0:T(8,128)(2,1)S(1)} %copy-done.1), custom_call_target="tpu_custom_call" | custom-call | flops 6370099200 | bytes 18339840 | tf_op jit(solution)/shard_map/pallas_call | solution.py:62
  (12 shorter events, 0.1 us)
Async XLA Ops:
  7.2 1.4 copy-start
  27.9 72.8 %all-to-all-start = ((bf16[8,90,32,96]{3,2,1,0:T(8,128)(2,1)}), bf16[8,90,32,96]{3,2,1,0:T(8,128)(2,1)}, u32[]{:S(2)}, u32[]{:S(2)}) async-start(bf16[8,90,32,96]{3,2,1,0:T(8,128)(2,1)} %shard_map.86), calls=%async_computation | async-start | bytes 11796480 | tf_op jit(solution)/shard_map/all_to_all | solution.py:257
  158.4 26.1 %all-to-all-start.2 = ((bf16[256,8,384]{2,1,0:T(8,128)(2,1)}), bf16[256,8,384]{2,1,0:T(8,128)(2,1)}, u32[]{:S(2)}, u32[]{:S(2)}) async-start(bf16[256,8,384]{2,1,0:T(8,128)(2,1)} %copy.39), calls=%async_computation.2 | async-start | bytes 3145728 | tf_op jit(solution)/shard_map/all_to_all | solution.py:257
  172.9 3.7 copy-start.2
  217.5 199.8 %all-to-all-start.4 = ((bf16[8,90,32,384]{3,2,1,0:T(8,128)(2,1)}), bf16[8,90,32,384]{3,2,1,0:T(8,128)(2,1)}, u32[]{:S(2)}, u32[]{:S(2)}) async-start(bf16[8,90,32,384]{3,2,1,0:T(8,128)(2,1)} %shard_map.87), calls=%async_computation.4 | async-start | bytes 35389440 | tf_op jit(solution)/shard_map/all_to_all | solution.py:257
  223.5 236.8 %all-gather.2.cloned.1.call-start = ((), (), s32[]{:S(2)}) async-start(), calls=%async_computation.11 | async-start | bytes 7864320 | tf_op jit(solution)/shard_map/all_gather | solution.py:292
  224.3 344.2 %reduce-scatter.2.cloned.1.call-start = ((), (), s32[]{:S(2)}) async-start(), calls=%async_computation.12 | async-start | bytes 7864320 | tf_op jit(solution)/shard_map/reduce_scatter | solution.py:297
  568.5 26.9 %copy-start.4 = (bf16[32,192,192]{2,1,0:T(8,128)(2,1)S(1)}, bf16[32,192,192]{2,1,0:T(8,128)(2,1)}, u32[]{:S(2)}) copy-start(bf16[32,192,192]{2,1,0:T(8,128)(2,1)} %get-tuple-element.14) | copy-start | bytes 7077892
  568.5 26.9 %copy-start.5 = (bf16[32,192,192]{2,1,0:T(8,128)(2,1)S(1)}, bf16[32,192,192]{2,1,0:T(8,128)(2,1)}, u32[]{:S(2)}) copy-start(bf16[32,192,192]{2,1,0:T(8,128)(2,1)} %get-tuple-element.15) | copy-start | bytes 7077892
  636.1 40.6 %all-to-all-start.7 = ((bf16[32,256,96]{1,2,0:T(8,128)(2,1)}), bf16[32,256,96]{1,2,0:T(8,128)(2,1)S(1)}, u32[]{:S(2)}, u32[]{:S(2)}) async-start(bf16[32,256,96]{1,2,0:T(8,128)(2,1)} %bitcast.18), calls=%async_computation.8 | async-start | bytes 3145728 | tf_op jit(solution)/shard_map/all_to_all | solution.py:257
  676.8 1.1 copy-start.3
  677.9 199.6 %all-to-all-start.9 = ((bf16[8,90,32,384]{3,2,1,0:T(8,128)(2,1)}), bf16[8,90,32,384]{3,2,1,0:T(8,128)(2,1)}, u32[]{:S(2)}, u32[]{:S(2)}) async-start(bf16[8,90,32,384]{3,2,1,0:T(8,128)(2,1)} %bitcast.49), calls=%async_computation.10 | async-start | bytes 35389440 | tf_op jit(solution)/shard_map/all_to_all | solution.py:257
  877.5 72.1 %all-to-all-start.8 = ((bf16[8,90,32,96]{3,2,1,0:T(8,128)(2,1)}), bf16[8,90,32,96]{3,2,1,0:T(8,128)(2,1)}, u32[]{:S(2)}, u32[]{:S(2)}) async-start(bf16[8,90,32,96]{3,2,1,0:T(8,128)(2,1)} %bitcast.50), calls=%async_computation.9 | async-start | bytes 11796480 | tf_op jit(solution)/shard_map/all_to_all | solution.py:257
  913.9 35.7 %copy-start.1 = (bf16[512,1440]{1,0:T(8,128)(2,1)S(1)}, bf16[512,1440]{1,0:T(8,128)(2,1)}, u32[]{:S(2)}) copy-start(bf16[512,1440]{1,0:T(8,128)(2,1)} %constant.22.table_ref) | copy-start | bytes 4423684
Sparse Core Ops, SparseCore 0:
  225.9 114.8 all-gather.1
  460.5 107.9 reduce-scatter.1

commit v3 on v2

--- a/solution.py
+++ b/solution.py
@@ -297,6 +297,7 @@
     coefficients = lax.psum_scatter(coefficients, "azimuth", scatter_dimension=0, tiled=True)
     grad_rows = synthesis(grad_modes, forward_legendre)
     grad_rows = exchange(grad_rows.reshape(polar, lat, orders, 2 * C), "polar")
+    coefficients, grad_rows = lax.optimization_barrier((coefficients, grad_rows))
 
     coefficients = exchange(coefficients.transpose(1, 0, 2), "polar")
     mixed = dot32("slmk,lkj->slmj", coefficients.reshape(polar, depth, mine, 2 * C), kernel)

time: 979 us -> 915 us (0.935)
  waiting for transfers between devices: 515 us -> 418 us
  blocking collectives: 111 us -> 149 us
    all_to_all x6 -> x5, waiting for transfers between devices: 406 us -> 304 us  [exchange(): return lax.all_to_all(blocks, axis, split_axis=0, concat_axis=0, tiled=True)]
    all_to_all x4 -> x5, blocking collectives: 111 us -> 149 us  [exchange(): return lax.all_to_all(blocks, axis, split_axis=0, concat_axis=0, tiled=True)]
    all_to_all x6 -> x5, starting transfers between devices: 30.9 us -> 26.6 us  [exchange(): return lax.all_to_all(blocks, axis, split_axis=0, concat_axis=0, tiled=True)]
  transfers between devices with their start and end apart: 8 -> 7, of which waited for: 7 -> 6; matrix products, arithmetic and copies ran while one was open for 6% -> 6% of each run, Pallas kernels for 16% -> 12%
where the time goes in v3:
time: 915 us; the launch traced here: 912 us
  waiting for transfers between devices  418 us (46%)
  Pallas kernels  210 us (23%)
  blocking collectives  149 us (16%)
  local copies, waits for them, and re-layouts  77.1 us (8%)
  starting transfers between devices  26.9 us (3%)
  between operations  14.2 us (2%)
  matrix products  13.5 us (1%)
    all_to_all x5, waiting for transfers between devices, exchange(): return lax.all_to_all(blocks, axis, split_axis=0, concat_axis=0, tiled=True)  304 us
    all_to_all x5, blocking collectives, exchange(): return lax.all_to_all(blocks, axis, split_axis=0, concat_axis=0, tiled=True)  149 us
    reduce_scatter x1, waiting for transfers between devices, on_device(): lax.psum_scatter(coefficients, 'azimuth', scatter_dimension=0, tiled=True)  113 us
    pallas_call x4, Pallas kernels, call_rows(): pl.pallas_call(body, grid=(out_shape[out_axis] // step,), in_specs=[block...  106 us
    pallas_call x2, Pallas kernels, analysis(): pl.pallas_call(body, grid=(orders // block, rows // step), in_specs=[pl.B...  59.1 us
    pallas_call x2, Pallas kernels, synthesis(): pl.pallas_call(body, grid=(orders // block, rows // step), in_specs=[pl.B...  45.1 us
    all_to_all x5, starting transfers between devices, exchange(): return lax.all_to_all(blocks, axis, split_axis=0, concat_axis=0, tiled=True)  26.6 us
    reshape x1, local copies, waits for them, and re-layouts, on_device(): return (filtered, grid_grad.reshape(lat, lon * C))  21.4 us
  transfers between devices with their start and end apart: 7, of which 6 were waited for; matrix products, arithmetic and copies ran while one was open for 6% of the time, Pallas kernels for 12%

profile of v3, /device:TPU:0, one launch (start us, length us, event | category | flops | bytes accessed | tf_op | source)
XLA Modules:
  0.0 911.8 jit_solution(12028543569484543942)
XLA Ops:
  7.2 1.4 copy-done
  8.6 19.3 %shard_map.86 = bf16[8,90,32,96]{3,2,1,0:T(8,128)(2,1)} custom-call(bf16[90,48,1440]{2,1,0:T(8,128)(2,1)} %x_ref.1, bf16[512,1440]{1,0:T(8,128)(2,1)S(1)} %copy-done), custom_call_target="tpu_custom_call" | custom-call | flops 6370099200 | bytes 18339840 | tf_op jit(solution)/shard_map/pallas_call | solution.py:62
  27.9 5.2 all-to-all-start
  33.0 19.0 %reshape.47.x_ref = bf16[90,360,192]{2,1,0:T(8,128)(2,1)} reshape(bf16[90,69120]{1,0:T(8,128)(2,1)} %param.7) | data formatting | bytes 24883200 | tf_op jit(solution)/shard_map/reshape | solution.py:274
  52.1 1.0 dynamic-slice_bitcast_fusion
  53.1 0.2 copy.37.table_ref
  53.3 35.5 %shard_map.87 = bf16[8,90,32,384]{3,2,1,0:T(8,128)(2,1)} custom-call(bf16[90,360,192]{2,1,0:T(8,128)(2,1)} %reshape.47.x_ref, bf16[512,360]{1,0:T(8,128)(2,1)S(1)} %copy.37.table_ref), custom_call_target="tpu_custom_call" | custom-call | flops 6370099200 | bytes 30504960 | tf_op jit(solution)/shard_map/pallas_call | solution.py:62
  88.9 11.8 %all-to-all-done = bf16[8,90,32,96]{3,2,1,0:T(8,128)(2,1)} async-done(((bf16[8,90,32,96]{3,2,1,0:T(8,128)(2,1)}), bf16[8,90,32,96]{3,2,1,0:T(8,128)(2,1)}, u32[]{:S(2)}, u32[]{:S(2)}) %all-to-all-start) | async-done | bytes 4423712 | tf_op jit(solution)/shard_map/all_to_all | solution.py:257
  100.7 16.0 %shard_map.88 = bf16[32,96,256]{2,1,0:T(8,128)(2,1)S(1)} custom-call(bf16[720,32,96]{2,1,0:T(8,128)(2,1)} %bitcast.5.s_ref, bf16[720,32,256]{2,1,0:T(8,128)(2,1)} %f_ref.7), custom_call_target="tpu_custom_call" | custom-call | flops 1132462080 | bytes 16220160 | tf_op jit(solution)/shard_map/pallas_call | solution.py:190
  116.7 39.4 %all_to_all.50 = bf16[32,96,256]{2,1,0:T(8,128)(2,1)S(1)} all-to-all(bf16[32,96,256]{2,1,0:T(8,128)(2,1)S(1)} %shard_map.88), channel_id=1, replica_groups=mesh['polar'=8,'azimuth'=4] {'azimuth'}, dimensions={0} | all-to-all | bytes 3145728 | tf_op jit(solution)/shard_map/all_to_all | solution.py:257
  156.2 0.1 copy.38
  156.3 2.1 copy.39
  158.4 5.0 all-to-all-start.2
  163.4 9.6 %reshape.46 = bf16[32,2,192,192]{3,2,1,0:T(8,128)(2,1)} reshape(bf16[32,73728]{1,0:T(8,128)(2,1)} %param.11) | data formatting | bytes 9437184 | tf_op jit(solution)/shard_map/reshape | solution.py:278
  172.9 2.2 fusion.14
  175.2 1.5 copy-done.2
  176.7 3.1 slice_bitcast_fusion
  179.8 4.8 all-to-all-done.2
  184.5 8.1 fusion.9
  192.6 0.2 copy.41
  192.8 23.4 %all_to_all.51 = bf16[8,32,8,384]{3,2,1,0:T(8,128)(2,1)S(1)} all-to-all(bf16[8,32,8,384]{3,2,1,0:T(8,128)(2,1)S(1)} %copy.41), channel_id=1, replica_groups=mesh['polar'=8,'azimuth'=4] {'polar'}, dimensions={0} | all-to-all | bytes 3145728 | tf_op jit(solution)/shard_map/all_to_all | solution.py:257
  216.2 1.3 copy.60
  217.5 6.0 all-to-all-start.4
  223.5 0.0 all-gather.2.cloned.1.call-start
  223.6 0.7 all-gather.2.cloned.1.call-update
  224.2 193.0 %all-to-all-done.4 = bf16[8,90,32,384]{3,2,1,0:T(8,128)(2,1)} async-done(((bf16[8,90,32,384]{3,2,1,0:T(8,128)(2,1)}), bf16[8,90,32,384]{3,2,1,0:T(8,128)(2,1)}, u32[]{:S(2)}, u32[]{:S(2)}) %all-to-all-start.4) | async-done | bytes 17694752 | tf_op jit(solution)/shard_map/all_to_all | solution.py:257
  417.3 43.0 %shard_map.89 = bf16[32,256,384]{2,1,0:T(8,128)(2,1)} custom-call(bf16[720,32,384]{2,1,0:T(8,128)(2,1)} %bitcast.13.s_ref, bf16[720,32,256]{2,1,0:T(8,128)(2,1)} %f_ref.6), custom_call_target="tpu_custom_call" | custom-call | flops 4529848320 | bytes 29491200 | tf_op jit(solution)/shard_map/pallas_call | solution.py:190
  460.3 29.8 %shard_map.90 = bf16[720,32,384]{2,1,0:T(8,128)(2,1)} custom-call(bf16[32,256,384]{2,1,0:T(8,128)(2,1)} %all-gather.2.cloned.1.call-done.g_ref, bf16[720,32,256]{2,1,0:T(8,128)(2,1)} %f_ref.6), custom_call_target="tpu_custom_call" | custom-call | flops 4529848320 | bytes 29491200 | tf_op jit(solution)/shard_map/pallas_call | solution.py:234
  490.1 5.8 all-to-all-start.5
  495.9 0.3 reduce-scatter.2.cloned.1.call-start
  496.2 0.5 reduce-scatter.2.cloned.1.call-update
  496.7 113.2 %reduce-scatter.2.cloned.1.call-done = bf16[8,256,384]{2,1,0:T(8,128)(2,1)} async-done(((bf16[32,256,384]{2,1,0:T(8,128)(2,1)}), bf16[8,256,384]{2,1,0:T(8,128)(2,1)}) %reduce-scatter.2.cloned.1.call-update) | async-done | bytes 1572880 | tf_op jit(solution)/shard_map/reduce_scatter | solution.py:297
  609.9 79.8 %all-to-all-done.5.g_ref = bf16[8,90,32,384]{3,2,1,0:T(8,128)(2,1)} async-done(((bf16[8,90,32,384]{3,2,1,0:T(8,128)(2,1)}), bf16[8,90,32,384]{3,2,1,0:T(8,128)(2,1)}, u32[]{:S(2)}, u32[]{:S(2)}) %all-to-all-start.5) | async-done | bytes 17694752 | tf_op jit(solution)/shard_map/all_to_all | solution.py:257
  689.7 2.5 copy.43
  692.2 23.4 %all_to_all.52 = bf16[256,8,384]{2,1,0:T(8,128)(2,1)S(1)} all-to-all(bf16[256,8,384]{2,1,0:T(8,128)(2,1)S(1)} %copy.43), channel_id=1, replica_groups=mesh['polar'=8,'azimuth'=4] {'polar'}, dimensions={0} | all-to-all | bytes 3145728 | tf_op jit(solution)/shard_map/all_to_all | solution.py:257
  715.6 5.5 fusion.6
  721.1 0.2 copy.45
  721.3 23.4 %all_to_all.53 = bf16[8,32,8,384]{3,2,1,0:T(8,128)(2,1)S(1)} all-to-all(bf16[8,32,8,384]{3,2,1,0:T(8,128)(2,1)S(1)} %copy.45), channel_id=1, replica_groups=mesh['polar'=8,'azimuth'=4] {'polar'}, dimensions={0} | all-to-all | bytes 3145728 | tf_op jit(solution)/shard_map/all_to_all | solution.py:257
  744.7 4.6 reshape.56
  749.3 5.9 copy.46
  755.1 39.8 %all_to_all.54 = bf16[32,256,96]{1,2,0:T(8,128)(2,1)} all-to-all(bf16[32,256,96]{1,2,0:T(8,128)(2,1)S(1)} %bitcast.56), channel_id=1, replica_groups=mesh['polar'=8,'azimuth'=4] {'azimuth'}, dimensions={0} | all-to-all | bytes 3145728 | tf_op jit(solution)/shard_map/all_to_all | solution.py:257
  794.9 3.1 copy.47.g_ref
  798.0 15.3 %shard_map.91 = bf16[720,32,96]{2,1,0:T(8,128)(2,1)} custom-call(bf16[32,256,96]{2,1,0:T(8,128)(2,1)S(1)} %copy.47.g_ref, bf16[720,32,256]{2,1,0:T(8,128)(2,1)} %f_ref.7), custom_call_target="tpu_custom_call" | custom-call | flops 1132462080 | bytes 16220160 | tf_op jit(solution)/shard_map/pallas_call | solution.py:234
  813.4 4.7 all-to-all-start.9
  818.1 31.6 %shard_map.93 = bf16[90,360,192]{2,1,0:T(8,128)(2,1)} custom-call(bf16[8,90,32,384]{3,2,1,0:T(8,128)(2,1)} %all-to-all-done.5.g_ref, bf16[360,512]{1,0:T(8,128)(2,1)S(1)} %get-tuple-element.20.table_ref), custom_call_target="tpu_custom_call" | custom-call | flops 6370099200 | bytes 30504960 | tf_op jit(solution)/shard_map/pallas_call | solution.py:62
  849.7 21.4 %reshape.59 = bf16[90,69120]{1,0:T(8,128)(2,1)} reshape(bf16[90,360,192]{2,1,0:T(8,128)(2,1)} %shard_map.93) | data formatting | bytes 24883200 | tf_op jit(solution)/shard_map/reshape | solution.py:310
  871.1 14.4 %all-to-all-done.9.g_ref = bf16[8,90,32,96]{3,2,1,0:T(8,128)(2,1)} async-done(((bf16[8,90,32,96]{3,2,1,0:T(8,128)(2,1)}), bf16[8,90,32,96]{3,2,1,0:T(8,128)(2,1)}, u32[]{:S(2)}, u32[]{:S(2)}) %all-to-all-start.9) | async-done | bytes 4423712 | tf_op jit(solution)/shard_map/all_to_all | solution.py:257
  885.5 19.5 %shard_map.92 = bf16[90,48,1440]{2,1,0:T(8,128)(2,1)} custom-call(bf16[8,90,32,96]{3,2,1,0:T(8,128)(2,1)} %all-to-all-done.9.g_ref, bf16[512,1440]{1,0:T(8,128)(2,1)S(1)} %copy-done.1), custom_call_target="tpu_custom_call" | custom-call | flops 6370099200 | bytes 18339840 | tf_op jit(solution)/shard_map/pallas_call | solution.py:62
  (9 shorter events, 0.0 us)
Async XLA Ops:
  7.2 1.4 copy-start
  27.9 72.8 %all-to-all-start = ((bf16[8,90,32,96]{3,2,1,0:T(8,128)(2,1)}), bf16[8,90,32,96]{3,2,1,0:T(8,128)(2,1)}, u32[]{:S(2)}, u32[]{:S(2)}) async-start(bf16[8,90,32,96]{3,2,1,0:T(8,128)(2,1)} %shard_map.86), calls=%async_computation | async-start | bytes 11796480 | tf_op jit(solution)/shard_map/all_to_all | solution.py:257
  158.4 26.1 %all-to-all-start.2 = ((bf16[256,8,384]{2,1,0:T(8,128)(2,1)}), bf16[256,8,384]{2,1,0:T(8,128)(2,1)}, u32[]{:S(2)}, u32[]{:S(2)}) async-start(bf16[256,8,384]{2,1,0:T(8,128)(2,1)} %copy.39), calls=%async_computation.2 | async-start | bytes 3145728 | tf_op jit(solution)/shard_map/all_to_all | solution.py:257
  172.9 3.7 copy-start.2
  217.5 199.8 %all-to-all-start.4 = ((bf16[8,90,32,384]{3,2,1,0:T(8,128)(2,1)}), bf16[8,90,32,384]{3,2,1,0:T(8,128)(2,1)}, u32[]{:S(2)}, u32[]{:S(2)}) async-start(bf16[8,90,32,384]{3,2,1,0:T(8,128)(2,1)} %shard_map.87), calls=%async_computation.4 | async-start | bytes 35389440 | tf_op jit(solution)/shard_map/all_to_all | solution.py:257
  223.5 236.8 %all-gather.2.cloned.1.call-start = ((), (), s32[]{:S(2)}) async-start(), calls=%async_computation.11 | async-start | bytes 7864320 | tf_op jit(solution)/shard_map/all_gather | solution.py:292
  490.1 199.6 %all-to-all-start.5 = ((bf16[8,90,32,384]{3,2,1,0:T(8,128)(2,1)}), bf16[8,90,32,384]{3,2,1,0:T(8,128)(2,1)}, u32[]{:S(2)}, u32[]{:S(2)}) async-start(bf16[8,90,32,384]{3,2,1,0:T(8,128)(2,1)} %bitcast.49), calls=%async_computation.6 | async-start | bytes 35389440 | tf_op jit(solution)/shard_map/all_to_all | solution.py:257
  495.9 114.0 %reduce-scatter.2.cloned.1.call-start = ((), (), s32[]{:S(2)}) async-start(), calls=%async_computation.12 | async-start | bytes 7864320 | tf_op jit(solution)/shard_map/reduce_scatter | solution.py:297
  689.7 25.9 %copy-start.3 = (bf16[32,192,192]{2,1,0:T(8,128)(2,1)S(1)}, bf16[32,192,192]{2,1,0:T(8,128)(2,1)}, u32[]{:S(2)}) copy-start(bf16[32,192,192]{2,1,0:T(8,128)(2,1)} %get-tuple-element.18) | copy-start | bytes 7077892
  689.7 25.9 %copy-start.4 = (bf16[32,192,192]{2,1,0:T(8,128)(2,1)S(1)}, bf16[32,192,192]{2,1,0:T(8,128)(2,1)}, u32[]{:S(2)}) copy-start(bf16[32,192,192]{2,1,0:T(8,128)(2,1)} %get-tuple-element.19) | copy-start | bytes 7077892
  813.4 72.1 %all-to-all-start.9 = ((bf16[8,90,32,96]{3,2,1,0:T(8,128)(2,1)}), bf16[8,90,32,96]{3,2,1,0:T(8,128)(2,1)}, u32[]{:S(2)}, u32[]{:S(2)}) async-start(bf16[8,90,32,96]{3,2,1,0:T(8,128)(2,1)} %bitcast.50), calls=%async_computation.10 | async-start | bytes 11796480 | tf_op jit(solution)/shard_map/all_to_all | solution.py:257
  849.7 35.7 %copy-start.1 = (bf16[512,1440]{1,0:T(8,128)(2,1)S(1)}, bf16[512,1440]{1,0:T(8,128)(2,1)}, u32[]{:S(2)}) copy-start(bf16[512,1440]{1,0:T(8,128)(2,1)} %constant.22.table_ref) | copy-start | bytes 4423684
Sparse Core Ops, SparseCore 0:
  225.9 114.8 all-gather.1
  499.7 110.2 reduce-scatter.1
